TPU v7x, 128 devices: a whole 4x4x4 slice. The times are simulated.
128 devices in a mesh: patch: 64 (over y, z_hi, x, core), chan: 2 (over z_lo).
Axes of the slice: x: 4, y: 4, z: 4 (z_hi: 2, z_lo: 2; z = z_hi * 2 + z_lo), core: 2. Of those that a mesh axis runs over, the one named last changes fastest.
Arguments:
- coarse_map: bfloat16 [131072, 256], P('patch', 'chan'), may hold values from -6 to 6
- skip_map: bfloat16 [524288, 256], P('patch', 'chan'), may hold values from -6 to 6
- coarse_values: bfloat16 [131072, 576], P('patch'), may hold values from -0.125 to 0.125
- coarse_columns: int32 [2048, 9], P('patch'), may hold values from 0 to 2047, as said below
- fine_values: bfloat16 [524288, 576], P('patch'), may hold values from -0.125 to 0.125
- fine_columns: int32 [8192, 9], P('patch'), may hold values from 0 to 8191, as said below
- coarse_weight: bfloat16 [4, 256, 256], P(None, 'chan'), may hold values from -0.1875 to 0.1875
- coarse_bias: float32 [256], P('chan'), may hold values from -3 to 3
- up_weight: bfloat16 [4, 256, 256], P(None, 'chan'), may hold values from -0.125 to 0.125
- skip_weight: bfloat16 [4, 256, 256], P(None, 'chan'), may hold values from -0.125 to 0.125
- fine_bias: float32 [256], P('chan'), may hold values from -3 to 3
Outputs:
- restored: bfloat16 [524288, 256], P('patch', 'chan')
Inputs may be any that keep to these rules, and one draw needn't show every extreme that they name: `coarse_columns`: each row r holds 9 distinct block indices of 0 to 2047, one of them r itself; each differs from r, cyclically modulo 2048, by at most 8, and that distance is reached. `fine_columns`: each row r holds 9 distinct block indices of 0 to 8191, one of them r itself; each differs from r, cyclically modulo 8192, by at most 16, and that distance is reached.
All inputs are finite; a program needn't handle non-finite values.
Results may differ from a plain program's by a relative error of at most 0.011.
Values may be sent and summed in bfloat16 or wider, within the bound.
A program may use at most 192 MiB of HBM per device.

v0:
```python
import jax
import jax.numpy as jnp
from jax import lax
from jax.sharding import PartitionSpec as P

B = 64
RIM_C = 8
TERMS = 4
RIM_F = 16


def with_halo(block, sides, width):
    for axis, dim in sides:
        count = lax.axis_size(axis)
        forward = [(i, i + 1) for i in range(count - 1)]
        forward.append((count - 1, 0))
        backward = [(target, source) for source, target in forward]
        low = lax.ppermute(
            lax.slice_in_dim(block, block.shape[dim] - width, None, axis=dim), axis, forward
        )
        high = lax.ppermute(lax.slice_in_dim(block, 0, width, axis=dim), axis, backward)
        block = jnp.concatenate([low, block, high], axis=dim)
    return block


def block_product(source, entries, block_index):
    channels = source.shape[1]
    row_width = entries.shape[1]
    row_count = block_index.shape[0]
    blocks = source.reshape(-1, B, channels)
    picked = blocks[block_index].reshape(row_count, row_width, channels)
    entry_rows = entries.reshape(row_count, B, row_width)
    result = jnp.einsum("rpq,rqc->rpc", entry_rows, picked, preferred_element_type=jnp.float32)
    return result.reshape(row_count * B, channels)


def extended_index(columns, reach):
    row_count = columns.shape[0]
    blocks_all = row_count * lax.axis_size("patch")
    device = lax.axis_index("patch")
    own_rows = device * row_count + jnp.arange(row_count, dtype=jnp.int32)
    offset = (columns - own_rows[:, None] + reach) % blocks_all - reach
    return jnp.arange(row_count, dtype=jnp.int32)[:, None] + reach + offset


def laplace(signal, entries, block_index, border):
    extended = border(signal)
    result = block_product(extended, entries, block_index)
    return result


def chebyshev(signal, entries, block_index, border):
    series = [signal]
    series.append(laplace(signal, entries, block_index, border).astype(jnp.bfloat16))
    for order in range(2, TERMS):
        newer = 2.0 * laplace(series[-1], entries, block_index, border) - series[-2].astype(
            jnp.float32
        )
        series.append(newer.astype(jnp.bfloat16))
    return series


def project(series, weight):
    result = jnp.dot(series[0], weight[0], preferred_element_type=jnp.float32)
    for order in range(1, len(series)):
        result = result + jnp.dot(series[order], weight[order], preferred_element_type=jnp.float32)
    return result


def per_device(
    coarse_map,
    skip_map,
    coarse_values,
    coarse_columns,
    fine_values,
    fine_columns,
    coarse_weight,
    coarse_bias,
    up_weight,
    skip_weight,
    fine_bias,
):
    coarse_index = extended_index(coarse_columns, RIM_C)
    fine_index = extended_index(fine_columns, RIM_F)

    def fine_border(signal):
        return with_halo(signal, (("patch", 0),), RIM_F * B)

    def coarse_border(signal):
        return with_halo(signal, (("patch", 0),), RIM_C * B)

    coarse_series = chebyshev(coarse_map, coarse_values, coarse_index, coarse_border)
    partial_terms = project(coarse_series, coarse_weight)
    summed = lax.psum_scatter(partial_terms, "chan", scatter_dimension=1, tiled=True)
    hidden = jnp.maximum(summed + coarse_bias, 0.0).astype(jnp.bfloat16)
    pixels, channels = hidden.shape
    upsampled = jnp.broadcast_to(hidden[:, None, :], (pixels, 4, channels)).reshape(
        pixels * 4, channels
    )
    joined = jnp.concatenate([upsampled, skip_map], axis=1)
    fine_series = chebyshev(joined, fine_values, fine_index, fine_border)
    weight_joined = jnp.concatenate([up_weight, skip_weight], axis=1)
    fine_terms = project(fine_series, weight_joined)
    restored = lax.psum_scatter(fine_terms, "chan", scatter_dimension=1, tiled=True)
    return (restored + fine_bias).astype(jnp.bfloat16)


def solution(mesh):
    placed = (
        P("patch", "chan"),
        P("patch", "chan"),
        P("patch", None),
        P("patch", None),
        P("patch", None),
        P("patch", None),
        P(None, "chan", None),
        P("chan"),
        P(None, "chan", None),
        P(None, "chan", None),
        P("chan"),
    )
    return jax.shard_map(
        per_device, mesh=mesh, in_specs=placed, out_specs=P("patch", "chan"), check_vma=False
    )
```

profile of v0, /device:TPU:0, one launch (start us, length us, event | category | flops | bytes accessed | tf_op | source)
XLA Modules:
  0.0 510.7 jit_solution(417702562062345417)
XLA Ops:
  6.5 1.0 fusion.30
  7.6 8.1 %collective-permute-start.1 = (bf16[512,128]{1,0:T(8,128)(2,1)S(1)}, bf16[512,128]{1,0:T(8,128)(2,1)}, u32[]{:S(2)}, u32[]{:S(2)}) collective-permute-start(bf16[512,128]{1,0:T(8,128)(2,1)S(1)} %get-tuple-element.16), channel_id=1, source_target_pairs={{2,0},{4,2},{6,4},{8,6},{10,8},{12,10},{14,12},{16,14},{18,16},{20... | collective-permute-start | bytes 393224 | tf_op jit(solution)/shard_map/ppermute | solution.py:21
  15.7 2.8 fusion.13
  18.5 0.7 compare_select_fusion.1
  19.4 3.1 copy.19
  22.5 1.2 pad_maximum_fusion.5
  23.7 13.3 %gather_fusion = bf16[288,64,128]{2,1,0:T(8,128)(2,1)} fusion(bf16[48,64,128]{2,1,0:T(8,128)(2,1)S(1)} %bitcast.124, s32[1024]{0:T(1024)S(1)} %pad_clamp_fusion.1), kind=kCustom, calls=%fused_computation | custom fusion | bytes 9438336 | tf_op jit(solution)/shard_map/gather | solution.py:31
  37.1 3.6 convolution_convert_fusion.1
  40.8 7.6 %collective-permute-start.3 = (bf16[512,128]{1,0:T(8,128)(2,1)S(1)}, bf16[512,128]{1,0:T(8,128)(2,1)S(1)}, u32[]{:S(2)}, u32[]{:S(2)}) collective-permute-start(bf16[512,128]{1,0:T(8,128)(2,1)S(1)} %bitcast.137), channel_id=1, source_target_pairs={{2,0},{4,2},{6,4},{8,6},{10,8},{12,10},{14,12},{16,14},{18,16},{20... | collective-permute-start | bytes 393224 | tf_op jit(solution)/shard_map/ppermute | solution.py:21
  48.4 2.6 convolution_add_fusion.5
  51.0 13.3 %gather_fusion.1 = bf16[288,64,128]{2,1,0:T(8,128)(2,1)} fusion(bf16[48,64,128]{2,1,0:T(8,128)(2,1)S(1)} %bitcast.125, s32[1024]{0:T(1024)S(1)} %pad_clamp_fusion.1), kind=kCustom, calls=%fused_computation.1 | custom fusion | bytes 9438336 | tf_op jit(solution)/shard_map/gather | solution.py:31
  64.4 3.5 convolution_multiply_fusion.1
  68.0 0.1 fusion.7
  68.2 7.8 %collective-permute-start.5 = (bf16[512,128]{1,0:T(8,128)(2,1)S(1)}, bf16[512,128]{1,0:T(8,128)(2,1)S(1)}, u32[]{:S(2)}, u32[]{:S(2)}) collective-permute-start(bf16[512,128]{1,0:T(8,128)(2,1)S(1)} %get-tuple-element.12), channel_id=1, source_target_pairs={{2,0},{4,2},{6,4},{8,6},{10,8},{12,10},{14,12},{16,14},{18,16},{20... | collective-permute-start | bytes 393224 | tf_op jit(solution)/shard_map/ppermute | solution.py:21
  76.0 2.6 convolution_add_fusion.4
  78.6 13.3 %gather_fusion.2 = bf16[288,64,128]{2,1,0:T(8,128)(2,1)} fusion(bf16[48,64,128]{2,1,0:T(8,128)(2,1)S(1)} %bitcast.123, s32[1024]{0:T(1024)S(1)} %pad_clamp_fusion.1), kind=kCustom, calls=%fused_computation.2 | custom fusion | bytes 9438336 | tf_op jit(solution)/shard_map/gather | solution.py:31
  92.0 3.7 fusion.6
  95.7 2.6 convolution_add_fusion.3
  98.4 0.1 copy.20
  98.5 0.2 reshape.135
  98.8 13.6 %copy.21 = bf16[8192,576]{1,0:T(8,128)(2,1)} copy(bf16[8192,576]{0,1:T(8,128)(2,1)} %param.15) | data formatting | bytes 18874368 | tf_op args[4]
  112.5 21.7 %reduce-scatter.3.cloned.1.call-done = f32[2048,128]{1,0:T(8,128)} async-done(((f32[2048,256]{1,0:T(8,128)}), f32[2048,128]{1,0:T(8,128)}) %reduce-scatter.3.cloned.1.call-update) | async-done | bytes 1048592 | tf_op jit(solution)/shard_map/reduce_scatter | solution.py:94
  134.2 1.5 maximum_convert_fusion
  135.7 0.6 broadcast_in_dim.7
  136.3 1.1 fusion.8
  137.5 7.8 %collective-permute-start.7 = (bf16[1024,256]{1,0:T(8,128)(2,1)S(1)}, bf16[1024,256]{1,0:T(8,128)(2,1)S(1)}, u32[]{:S(2)}, u32[]{:S(2)}) collective-permute-start(bf16[1024,256]{1,0:T(8,128)(2,1)S(1)} %get-tuple-element.10), channel_id=1, source_target_pairs={{2,0},{4,2},{6,4},{8,6},{10,8},{12,10},{14,12},{16,14},{18,16},{20... | collective-permute-start | bytes 1572872 | tf_op jit(solution)/shard_map/ppermute | solution.py:21
  145.4 4.5 fusion.3
  149.9 2.0 collective-permute-done.6
  151.9 0.2 collective-permute-done.7
  152.1 15.8 %pad_maximum_fusion.1 = bf16[10240,256]{1,0:T(8,128)(2,1)} fusion(bf16[1024,256]{1,0:T(8,128)(2,1)S(1)} %collective-permute-done.7, bf16[8192,128]{1,0:T(8,128)(2,1)S(1)} %copy-done.2, bf16[8192,128]{1,0:T(8,128)(2,1)S(1)} %bitcast.116, bf16[1024,256]{1,0:T(8,128)(2,1)S(1)} %collective-permute-done.6), kind=kLoop, calls=%fused_computation.20 | loop fusion | flops 20971520 | bytes 10485760 | tf_op jit(solution)/shard_map/concatenate | solution.py:22
  167.9 29.7 %gather_fusion.3 = bf16[1152,64,256]{2,1,0:T(8,128)(2,1)} fusion(bf16[160,64,256]{2,1,0:T(8,128)(2,1)} %bitcast.101, s32[2048]{0:T(1024)S(1)} %pad_clamp_fusion), kind=kCustom, calls=%fused_computation.3 | custom fusion | bytes 75502080 | tf_op jit(solution)/shard_map/gather | solution.py:31
  197.6 20.7 %convolution_convert_fusion = bf16[128,256,64]{1,2,0:T(8,128)(2,1)} fusion(bf16[128,64,576]{2,1,0:T(8,128)(2,1)} %bitcast.103, bf16[128,576,256]{2,1,0:T(8,128)(2,1)} %bitcast.106), kind=kOutput, calls=%fused_computation.29 | convolution fusion | flops 2418016256 | bytes 51380224 | tf_op jit(solution)/shard_map/rpq,rqc->rpc/dot_general | solution.py:33
  218.2 1.3 fusion.27
  219.6 7.9 %collective-permute-start.9 = (bf16[1024,256]{1,0:T(8,128)(2,1)S(1)}, bf16[1024,256]{1,0:T(8,128)(2,1)S(1)}, u32[]{:S(2)}, u32[]{:S(2)}) collective-permute-start(bf16[1024,256]{1,0:T(8,128)(2,1)S(1)} %bitcast.135), channel_id=1, source_target_pairs={{2,0},{4,2},{6,4},{8,6},{10,8},{12,10},{14,12},{16,14},{18,16},{20... | collective-permute-start | bytes 1572872 | tf_op jit(solution)/shard_map/ppermute | solution.py:21
  227.5 9.3 %convolution_add_fusion.2 = f32[8192,256]{1,0:T(8,128)} fusion(f32[8192,256]{1,0:T(8,128)} %fusion.3, bf16[8192,256]{1,0:T(8,128)(2,1)} %bitcast.110, bf16[4,256,256]{2,1,0:T(8,128)(2,1)S(1)} %constant_dynamic-update-slice_fusion), kind=kOutput, calls=%fused_computation.8 | convolution fusion | flops 1075838976 | bytes 21102592 | tf_op jit(solution)/shard_map/dot_general | solution.py:66
  236.8 15.8 %pad_maximum_fusion.2 = bf16[10240,256]{1,0:T(8,128)(2,1)} fusion(bf16[1024,256]{1,0:T(8,128)(2,1)S(1)} %collective-permute-done.9, bf16[8192,256]{1,0:T(8,128)(2,1)S(1)} %bitcast.111, bf16[1024,256]{1,0:T(8,128)(2,1)S(1)} %collective-permute-done.8), kind=kLoop, calls=%fused_computation.21 | loop fusion | flops 15728640 | bytes 10485760 | tf_op jit(solution)/shard_map/concatenate | solution.py:22
  252.7 29.7 %gather_fusion.4 = bf16[1152,64,256]{2,1,0:T(8,128)(2,1)} fusion(bf16[160,64,256]{2,1,0:T(8,128)(2,1)} %bitcast.102, s32[2048]{0:T(1024)S(1)} %pad_clamp_fusion), kind=kCustom, calls=%fused_computation.4 | custom fusion | bytes 75502080 | tf_op jit(solution)/shard_map/gather | solution.py:31
  282.3 22.9 %fusion.2 = (bf16[128,64,256]{2,1,0:T(8,128)(2,1)}, f32[128,256,64]{1,2,0:T(8,128)}) fusion(bf16[128,64,128]{2,1,0:T(8,128)(2,1)} %bitcast.119, bf16[128,64,128]{2,1,0:T(8,128)(2,1)S(1)} %bitcast.117, bf16[128,64,576]{2,1,0:T(8,128)(2,1)} %bitcast.104, bf16[128,576,256]{2,1,0:T(8,128)(2,1)} %bitcast.107), kind=kOutput, calls=%fused_computation.14 | convolution fusion | flops 2430599168 | bytes 63963136 | tf_op jit(solution)/shard_map/rpq,rqc->rpc/dot_general | solution.py:33
  305.3 4.2 fusion
  309.6 7.6 %collective-permute-start.11 = (bf16[1024,256]{1,0:T(8,128)(2,1)S(1)}, bf16[1024,256]{1,0:T(8,128)(2,1)S(1)}, u32[]{:S(2)}, u32[]{:S(2)}) collective-permute-start(bf16[1024,256]{1,0:T(8,128)(2,1)S(1)} %get-tuple-element.6), channel_id=1, source_target_pairs={{2,0},{4,2},{6,4},{8,6},{10,8},{12,10},{14,12},{16,14},{18,16},{20... | collective-permute-start | bytes 1572872 | tf_op jit(solution)/shard_map/ppermute | solution.py:21
  317.3 4.5 convolution_add_fusion.1
  321.8 2.2 collective-permute-done.10
  324.0 15.8 %pad_maximum_fusion.3 = bf16[10240,256]{1,0:T(8,128)(2,1)} fusion(bf16[1024,256]{1,0:T(8,128)(2,1)S(1)} %collective-permute-done.11, bf16[8192,256]{1,0:T(8,128)(2,1)S(1)} %fusion, bf16[1024,256]{1,0:T(8,128)(2,1)S(1)} %collective-permute-done.10), kind=kLoop, calls=%fused_computation.22 | loop fusion | flops 15728640 | bytes 10485760 | tf_op jit(solution)/shard_map/concatenate | solution.py:22
  339.8 29.7 %gather_fusion.5 = bf16[1152,64,256]{2,1,0:T(8,128)(2,1)} fusion(bf16[160,64,256]{2,1,0:T(8,128)(2,1)} %bitcast.100, s32[2048]{0:T(1024)S(1)} %pad_clamp_fusion), kind=kCustom, calls=%fused_computation.5 | custom fusion | bytes 75502080 | tf_op jit(solution)/shard_map/gather | solution.py:31
  369.5 20.7 %fusion.1 = bf16[128,64,256]{2,1,0:T(8,128)(2,1)} fusion(bf16[128,64,576]{2,1,0:T(8,128)(2,1)} %bitcast.105, bf16[128,576,256]{2,1,0:T(8,128)(2,1)} %bitcast.108, bf16[128,256,64]{1,2,0:T(8,128)(2,1)} %convolution_convert_fusion), kind=kOutput, calls=%fused_computation.12 | convolution fusion | flops 2424307712 | bytes 55574528 | tf_op jit(solution)/shard_map/rpq,rqc->rpc/dot_general | solution.py:33
  390.2 6.7 %convolution_add_fusion = f32[8192,256]{1,0:T(8,128)} fusion(f32[8192,256]{1,0:T(8,128)S(1)} %copy-done.1, bf16[8192,256]{1,0:T(8,128)(2,1)} %bitcast.127, bf16[4,256,256]{2,1,0:T(8,128)(2,1)S(1)} %constant_dynamic-update-slice_fusion), kind=kOutput, calls=%fused_computation.6 | convolution fusion | flops 1075838976 | bytes 21102592 | tf_op jit(solution)/shard_map/dot_general | solution.py:66
  397.0 102.9 %reduce-scatter.5.cloned.1.call-done = f32[8192,128]{1,0:T(8,128)} async-done(((f32[8192,256]{1,0:T(8,128)}), f32[8192,128]{1,0:T(8,128)}) %reduce-scatter.5.cloned.1.call-update) | async-done | bytes 4194320 | tf_op jit(solution)/shard_map/reduce_scatter | solution.py:104
  499.9 3.7 add_convert_fusion
  (68 shorter events, 1.1 us)
Async XLA Ops:
  6.5 127.7 %reduce-scatter.3.cloned.1.call-start = ((), (), s32[]{:S(2)}) async-start(), calls=%async_computation.2 | async-start | bytes 3145728 | tf_op jit(solution)/shard_map/reduce_scatter | solution.py:94
  7.5 15.0 %collective-permute-start = (bf16[512,128]{1,0:T(8,128)(2,1)S(1)}, bf16[512,128]{1,0:T(8,128)(2,1)S(1)}, u32[]{:S(2)}, u32[]{:S(2)}) collective-permute-start(bf16[512,128]{1,0:T(8,128)(2,1)S(1)} %get-tuple-element.15), channel_id=1, source_target_pairs={{0,2},{2,4},{4,6},{6,8},{8,10},{10,12},{12,14},{14,16},{16,18},{18... | collective-permute-start | bytes 393224 | tf_op jit(solution)/shard_map/ppermute | solution.py:18
  7.6 14.9 %collective-permute-start.1 = (bf16[512,128]{1,0:T(8,128)(2,1)S(1)}, bf16[512,128]{1,0:T(8,128)(2,1)}, u32[]{:S(2)}, u32[]{:S(2)}) collective-permute-start(bf16[512,128]{1,0:T(8,128)(2,1)S(1)} %get-tuple-element.16), channel_id=1, source_target_pairs={{2,0},{4,2},{6,4},{8,6},{10,8},{12,10},{14,12},{16,14},{18,16},{20... | collective-permute-start | bytes 393224 | tf_op jit(solution)/shard_map/ppermute | solution.py:21
  37.1 11.3 %copy-start.8 = (f32[2048,256]{1,0:T(8,128)S(1)}, f32[2048,256]{1,0:T(8,128)}, u32[]{:S(2)}) copy-start(f32[2048,256]{1,0:T(8,128)} %fusion.13) | copy-start | bytes 6291460
  40.6 10.3 %copy-start.5 = (bf16[32,128,64]{1,2,0:T(8,128)(2,1)}, bf16[32,128,64]{1,2,0:T(8,128)(2,1)S(1)}, u32[]{:S(2)}) copy-start(bf16[32,128,64]{1,2,0:T(8,128)(2,1)S(1)} %convolution_convert_fusion.1) | copy-start | bytes 1572868
  40.7 10.3 %collective-permute-start.2 = (bf16[512,128]{1,0:T(8,128)(2,1)S(1)}, bf16[512,128]{1,0:T(8,128)(2,1)S(1)}, u32[]{:S(2)}, u32[]{:S(2)}) collective-permute-start(bf16[512,128]{1,0:T(8,128)(2,1)S(1)} %bitcast.138), channel_id=1, source_target_pairs={{0,2},{2,4},{4,6},{6,8},{8,10},{10,12},{12,14},{14,16},{16,18},{18... | collective-permute-start | bytes 393224 | tf_op jit(solution)/shard_map/ppermute | solution.py:18
  40.8 10.2 %collective-permute-start.3 = (bf16[512,128]{1,0:T(8,128)(2,1)S(1)}, bf16[512,128]{1,0:T(8,128)(2,1)S(1)}, u32[]{:S(2)}, u32[]{:S(2)}) collective-permute-start(bf16[512,128]{1,0:T(8,128)(2,1)S(1)} %bitcast.137), channel_id=1, source_target_pairs={{2,0},{4,2},{6,4},{8,6},{10,8},{12,10},{14,12},{16,14},{18,16},{20... | collective-permute-start | bytes 393224 | tf_op jit(solution)/shard_map/ppermute | solution.py:21
  64.4 3.6 copy-start.9
  64.4 11.6 %copy-start.6 = (f32[2048,256]{1,0:T(8,128)S(1)}, f32[2048,256]{1,0:T(8,128)}, u32[]{:S(2)}) copy-start(f32[2048,256]{1,0:T(8,128)} %convolution_add_fusion.5) | copy-start | bytes 6291460
  68.1 10.5 %collective-permute-start.4 = (bf16[512,128]{1,0:T(8,128)(2,1)S(1)}, bf16[512,128]{1,0:T(8,128)(2,1)S(1)}, u32[]{:S(2)}, u32[]{:S(2)}) collective-permute-start(bf16[512,128]{1,0:T(8,128)(2,1)S(1)} %get-tuple-element.11), channel_id=1, source_target_pairs={{0,2},{2,4},{4,6},{6,8},{8,10},{10,12},{12,14},{14,16},{16,18},{18... | collective-permute-start | bytes 393224 | tf_op jit(solution)/shard_map/ppermute | solution.py:18
  68.2 10.4 %collective-permute-start.5 = (bf16[512,128]{1,0:T(8,128)(2,1)S(1)}, bf16[512,128]{1,0:T(8,128)(2,1)S(1)}, u32[]{:S(2)}, u32[]{:S(2)}) collective-permute-start(bf16[512,128]{1,0:T(8,128)(2,1)S(1)} %get-tuple-element.12), channel_id=1, source_target_pairs={{2,0},{4,2},{6,4},{8,6},{10,8},{12,10},{14,12},{16,14},{18,16},{20... | collective-permute-start | bytes 393224 | tf_op jit(solution)/shard_map/ppermute | solution.py:21
  92.0 3.7 copy-start.7
  95.7 2.7 copy-start.12
  98.3 401.6 %reduce-scatter.5.cloned.1.call-start = ((), (), s32[]{:S(2)}) async-start(), calls=%async_computation.3 | async-start | bytes 12582912 | tf_op jit(solution)/shard_map/reduce_scatter | solution.py:104
  98.7 13.7 %copy-start.10 = (bf16[4,128,256]{2,1,0:T(8,128)(2,1)S(1)}, bf16[4,128,256]{2,1,0:T(8,128)(2,1)}, u32[]{:S(2)}) copy-start(bf16[4,128,256]{2,1,0:T(8,128)(2,1)} %param.19) | copy-start | bytes 786436
  98.7 13.7 %copy-start.11 = (bf16[4,128,256]{2,1,0:T(8,128)(2,1)S(1)}, bf16[4,128,256]{2,1,0:T(8,128)(2,1)}, u32[]{:S(2)}) copy-start(bf16[4,128,256]{2,1,0:T(8,128)(2,1)} %param.20) | copy-start | bytes 786436
  98.8 35.5 %copy-start.13 = (f32[128]{0:T(128)S(1)}, f32[128]{0:T(128)}, u32[]{:S(2)}) copy-start(f32[128]{0:T(128)} %param.18) | copy-start | bytes 1540
  134.2 11.2 %copy-start.2 = (bf16[8192,128]{1,0:T(8,128)(2,1)S(1)}, bf16[8192,128]{1,0:T(8,128)(2,1)}, u32[]{:S(2)}) copy-start(bf16[8192,128]{1,0:T(8,128)(2,1)} %param.12) | copy-start | bytes 6291460
  137.5 14.4 %collective-permute-start.6 = (bf16[1024,256]{1,0:T(8,128)(2,1)S(1)}, bf16[1024,256]{1,0:T(8,128)(2,1)S(1)}, u32[]{:S(2)}, u32[]{:S(2)}) collective-permute-start(bf16[1024,256]{1,0:T(8,128)(2,1)S(1)} %get-tuple-element.9), channel_id=1, source_target_pairs={{0,2},{2,4},{4,6},{6,8},{8,10},{10,12},{12,14},{14,16},{16,18},{18... | collective-permute-start | bytes 1572872 | tf_op jit(solution)/shard_map/ppermute | solution.py:18
  137.5 14.5 %collective-permute-start.7 = (bf16[1024,256]{1,0:T(8,128)(2,1)S(1)}, bf16[1024,256]{1,0:T(8,128)(2,1)S(1)}, u32[]{:S(2)}, u32[]{:S(2)}) collective-permute-start(bf16[1024,256]{1,0:T(8,128)(2,1)S(1)} %get-tuple-element.10), channel_id=1, source_target_pairs={{2,0},{4,2},{6,4},{8,6},{10,8},{12,10},{14,12},{16,14},{18,16},{20... | collective-permute-start | bytes 1572872 | tf_op jit(solution)/shard_map/ppermute | solution.py:21
  219.5 17.3 %collective-permute-start.8 = (bf16[1024,256]{1,0:T(8,128)(2,1)S(1)}, bf16[1024,256]{1,0:T(8,128)(2,1)S(1)}, u32[]{:S(2)}, u32[]{:S(2)}) collective-permute-start(bf16[1024,256]{1,0:T(8,128)(2,1)S(1)} %bitcast.136), channel_id=1, source_target_pairs={{0,2},{2,4},{4,6},{6,8},{8,10},{10,12},{12,14},{14,16},{16,18},{18... | collective-permute-start | bytes 1572872 | tf_op jit(solution)/shard_map/ppermute | solution.py:18
  219.6 17.2 %collective-permute-start.9 = (bf16[1024,256]{1,0:T(8,128)(2,1)S(1)}, bf16[1024,256]{1,0:T(8,128)(2,1)S(1)}, u32[]{:S(2)}, u32[]{:S(2)}) collective-permute-start(bf16[1024,256]{1,0:T(8,128)(2,1)S(1)} %bitcast.135), channel_id=1, source_target_pairs={{2,0},{4,2},{6,4},{8,6},{10,8},{12,10},{14,12},{16,14},{18,16},{20... | collective-permute-start | bytes 1572872 | tf_op jit(solution)/shard_map/ppermute | solution.py:21
  227.5 9.3 %copy-start = (bf16[128,256,64]{1,2,0:T(8,128)(2,1)S(1)}, bf16[128,256,64]{1,2,0:T(8,128)(2,1)}, u32[]{:S(2)}) copy-start(bf16[128,256,64]{1,2,0:T(8,128)(2,1)} %convolution_convert_fusion) | copy-start | bytes 12582916
  282.3 22.9 %copy-start.3 = (bf16[8192,128]{1,0:T(8,128)(2,1)S(1)}, bf16[8192,128]{1,0:T(8,128)(2,1)}, u32[]{:S(2)}) copy-start(bf16[8192,128]{1,0:T(8,128)(2,1)} %param.12) | copy-start | bytes 6291460
  305.3 12.0 %slice-start = ((s8[8388608]{0:T(1024)(128)(4,1)}), s8[4194304]{0:T(1024)(128)(4,1)S(1)}, s32[]{:S(2)}) async-start(s8[8388608]{0:T(1024)(128)(4,1)} %bitcast.112), calls=%async_computation.4 | async-start | bytes 8388608
  305.3 12.0 %slice-start.1 = ((s8[8388608]{0:T(1024)(128)(4,1)}), s8[4194304]{0:T(1024)(128)(4,1)S(1)}, s32[]{:S(2)}) async-start(s8[8388608]{0:T(1024)(128)(4,1)} %bitcast.112), calls=%async_computation.5 | async-start | bytes 8388608
  305.3 12.0 %copy-start.4 = (bf16[128,64,256]{2,1,0:T(8,128)(2,1)S(1)}, bf16[128,64,256]{2,1,0:T(8,128)(2,1)}, u32[]{:S(2)}) copy-start(bf16[128,64,256]{2,1,0:T(8,128)(2,1)} %get-tuple-element.17) | copy-start | bytes 12582916
  309.6 14.4 %collective-permute-start.10 = (bf16[1024,256]{1,0:T(8,128)(2,1)S(1)}, bf16[1024,256]{1,0:T(8,128)(2,1)S(1)}, u32[]{:S(2)}, u32[]{:S(2)}) collective-permute-start(bf16[1024,256]{1,0:T(8,128)(2,1)S(1)} %get-tuple-element.5), channel_id=1, source_target_pairs={{0,2},{2,4},{4,6},{6,8},{8,10},{10,12},{12,14},{14,16},{16,18},{18... | collective-permute-start | bytes 1572872 | tf_op jit(solution)/shard_map/ppermute | solution.py:18
  309.6 14.3 %collective-permute-start.11 = (bf16[1024,256]{1,0:T(8,128)(2,1)S(1)}, bf16[1024,256]{1,0:T(8,128)(2,1)S(1)}, u32[]{:S(2)}, u32[]{:S(2)}) collective-permute-start(bf16[1024,256]{1,0:T(8,128)(2,1)S(1)} %get-tuple-element.6), channel_id=1, source_target_pairs={{2,0},{4,2},{6,4},{8,6},{10,8},{12,10},{14,12},{16,14},{18,16},{20... | collective-permute-start | bytes 1572872 | tf_op jit(solution)/shard_map/ppermute | solution.py:21
  369.4 20.8 %copy-start.1 = (f32[8192,256]{1,0:T(8,128)S(1)}, f32[8192,256]{1,0:T(8,128)}, u32[]{:S(2)}) copy-start(f32[8192,256]{1,0:T(8,128)} %convolution_add_fusion.1) | copy-start | bytes 25165828
  396.9 103.0 %copy-start.14 = (f32[128]{0:T(128)S(1)}, f32[128]{0:T(128)}, u32[]{:S(2)}) copy-start(f32[128]{0:T(128)} %param.21) | copy-start | bytes 1540
Sparse Core Ops, SparseCore 0:
  98.4 35.7 reduce-scatter.2
  397.1 102.7 reduce-scatter.4
where the time goes:
time: 518 us; the launch traced here: 511 us
  local copies, waits for them, and re-layouts  149 us (29%)
  waiting for transfers between devices  129 us (25%)
  matrix products  111 us (21%)
  other arithmetic  60.1 us (12%)
  starting transfers between devices  47.4 us (9%)
  between operations  14 us (3%)
    gather x6, local copies, waits for them, and re-layouts, block_product(): picked = blocks[block_index].reshape(row_count, row_width, channels)  129 us
    reduce_scatter x1, waiting for transfers between devices, per_device(): lax.psum_scatter(fine_terms, 'chan', scatter_dimension=1, tiled=True)  103 us
    dot_general x6, matrix products, block_product(): jnp.einsum('rpq,rqc->rpc', entry_rows, picked, preferred_element_type=jnp...  75.1 us
    concatenate x6, other arithmetic, with_halo(): block = jnp.concatenate([low, block, high], axis=dim)  48.7 us
    ppermute x6, starting transfers between devices, with_halo(): lax.ppermute(lax.slice_in_dim(block, 0, width, axis=dim), axis, backward)  46.9 us
    dot_general x6, matrix products, project(): jnp.dot(series[order], weight[order], preferred_element_type=jnp.float32)  28.3 us
    reduce_scatter x1, waiting for transfers between devices, per_device(): lax.psum_scatter(partial_terms, 'chan', scatter_dimension=1, tiled=True)  21.7 us
    unnamed x37, local copies, waits for them, and re-layouts  16.8 us
  transfers between devices with their start and end apart: 14, of which 5 were waited for; matrix products, arithmetic and copies ran while one was open for 9% of the time, Pallas kernels for 0%

commit v1 on v0

v1 whole, which is shorter than its diff:
```python
import functools

import jax
import jax.numpy as jnp
from jax import lax
from jax.experimental import pallas as pl
from jax.experimental.pallas import tpu as pltpu
from jax.sharding import PartitionSpec as P

B = 64
NB = 9
RIM_C = 8
RIM_F = 16
TERMS = 4
FLIP = 8
F32 = jnp.float32
BF16 = jnp.bfloat16
MESH = pl.DeviceIdType.MESH


def dot(a, b):
    return jnp.dot(a, b, preferred_element_type=F32)


def place_of(offset, blocks_all, held):
    return jnp.minimum(lax.bitwise_and(offset, blocks_all - 1), held - 1)


def kernel(
    n_patch,
    cm,
    skip,
    vc_hbm,
    jc,
    vf_hbm,
    jf,
    wc_hbm,
    cb_hbm,
    up_hbm,
    sw_hbm,
    fb,
    out_hbm,
    cm_own,
    cm_oth,
    vc,
    wc,
    cb,
    up,
    sw,
    skip_own,
    skip_oth,
    vf,
    ce3,
    ce2,
    ce1,
    gc,
    hidden,
    g,
    b3,
    b2,
    b1,
    lo3,
    lo2,
    lo1,
    hi3,
    hi2,
    hi1,
    out,
    vct,
    vft,
    load_sem,
    vf_sem,
    gather_sem,
    skip_sem,
    halo_c_sem,
    halo_f_sem,
    out_sem,
):
    p = lax.axis_index("patch")
    c = lax.axis_index("chan")
    left = (lax.rem(p + n_patch - 1, n_patch), c)
    right = (lax.rem(p + 1, n_patch), c)
    partner = (p, 1 - c)
    z_hi = lax.rem(p // FLIP, 2)
    far = (p + FLIP - 2 * FLIP * z_hi, 1 - c)

    n_c = vc.shape[0]
    n_f = vf.shape[0]
    all_c = n_c * n_patch
    all_f = n_f * n_patch
    half = cm.shape[1]
    full = 2 * half

    def remote(src, dst, sems, target):
        return pltpu.make_async_remote_copy(
            src_ref=src,
            dst_ref=dst,
            send_sem=sems.at[0],
            recv_sem=sems.at[1],
            device_id=target,
            device_id_type=MESH,
        )

    own_rows = pl.ds(pl.multiple_of(c * half, half), half)
    own_cols = own_rows
    far_cols = pl.ds(pl.multiple_of((1 - c) * half, half), half)

    pairs = [
        (cm, cm_own),
        (wc_hbm, wc.at[:, pl.ds(0, half), :]),
        (cb_hbm, cb.at[c]),
        (vc_hbm, vct),
        (up_hbm.at[:, :, own_cols], up.at[:, own_rows, :]),
        (sw_hbm.at[:, :, own_cols], sw.at[:, pl.ds(0, half), :]),
        (skip, skip_own),
    ]
    loads = [pltpu.make_async_copy(a, b, load_sem.at[i]) for i, (a, b) in enumerate(pairs)]
    for load in loads:
        load.start()

    lanes = 128
    v_cols = vft.shape[2]
    v_parts = n_f * B // v_cols

    def vf_load(i, slot):
        cols = pl.ds(pl.multiple_of(i * v_cols, v_cols), v_cols)
        return pltpu.make_async_copy(vf_hbm.at[:, cols], vft.at[slot], vf_sem.at[slot])

    vf_load(0, 0).start()
    vf_load(1, 1).start()

    def turn_coarse():
        for t in range(n_c * B // lanes):
            value = vct[:, t * lanes : (t + 1) * lanes].T
            vc[pl.ds(t * (lanes // B), lanes // B)] = value.reshape(lanes // B, B, value.shape[1])

    def turn_fine(start, stop):
        @pl.loop(start // 2, stop // 2)
        def _(pair):
            for slot in range(2):
                i = 2 * pair + slot
                vf_load(i, slot).wait()
                for t in range(v_cols // lanes):
                    value = vft[slot, :, t * lanes : (t + 1) * lanes].T
                    blocks = pl.ds(i * (v_cols // B) + t * (lanes // B), lanes // B)
                    vf[blocks] = value.reshape(lanes // B, B, value.shape[1])

                @pl.when(i + 2 < v_parts)
                def _():
                    vf_load(i + 2, slot).start()

    with jax.named_scope("enter"):
        barrier = pltpu.get_barrier_semaphore()
        for target in (left, right, partner, far):
            pl.semaphore_signal(barrier, inc=1, device_id=target, device_id_type=MESH)
        pl.semaphore_wait(barrier, 4)

    cm_copy = remote(cm, cm_oth, gather_sem.at[0], partner)
    wc_copy = remote(wc_hbm, wc.at[:, pl.ds(half, half), :], gather_sem.at[1], far)
    cb_copy = remote(cb_hbm, cb.at[c], gather_sem.at[2], far)
    up_copy = remote(up_hbm.at[:, :, far_cols], up.at[:, own_rows, :], gather_sem.at[3], far)
    sw_copy = remote(
        sw_hbm.at[:, :, far_cols], sw.at[:, pl.ds(half, half), :], gather_sem.at[4], far
    )
    gathers = [cm_copy, wc_copy, cb_copy, up_copy, sw_copy]
    for copy in gathers:
        copy.start()

    chunk = 8
    steps = n_f // chunk
    rows = chunk * B

    def skip_copy(q):
        part = pl.ds(pl.multiple_of(q * rows, rows), rows)
        return remote(skip.at[part], skip_oth.at[part], skip_sem.at[q], partner)

    with jax.named_scope("wait coarse map"):
        for load in loads[:4]:
            load.wait()
        turn_coarse()
        for copy in (wc_copy, cb_copy, cm_copy):
            copy.wait_recv()
        cm_copy.wait_send()

    @pl.loop(0, steps // 2)
    def _(q):
        skip_copy(q).start()
        skip_copy(steps - 1 - q).start()

    cchunk = 4
    crows = cchunk * B

    def coarse_g(q, k):
        part = pl.ds(pl.multiple_of(q * crows, crows), crows)
        x = jnp.concatenate([cm_own[part, :], cm_oth[part, :]], axis=1)
        return dot(x, wc[k])

    def coarse_first(q):
        blocks = pl.ds(RIM_C + q * cchunk, cchunk)
        ce3[blocks] = coarse_g(q, 3).astype(BF16).reshape(cchunk, B, full)

    def coarse_halo(i, ext):
        sems = halo_c_sem.at[i]
        to_left = remote(
            ext.at[pl.ds(RIM_C, RIM_C)], ext.at[pl.ds(n_c + RIM_C, RIM_C)], sems.at[0], left
        )
        to_right = remote(ext.at[pl.ds(n_c, RIM_C)], ext.at[pl.ds(0, RIM_C)], sems.at[1], right)
        return to_left, to_right

    with jax.named_scope("coarse first"):
        coarse_first(0)
        coarse_first(1)
        coarse_first(n_c // cchunk - 2)
        coarse_first(n_c // cchunk - 1)
        halos = [coarse_halo(0, ce3)]
        for copy in halos[-1]:
            copy.start()

        @pl.loop(2, n_c // cchunk - 2)
        def _(q):
            coarse_first(q)

    with jax.named_scope("coarse g"):
        @pl.loop(0, n_c // cchunk)
        def _(q):
            part = pl.ds(pl.multiple_of(q * cchunk, cchunk), cchunk)
            for k in range(TERMS - 1):
                gc[k, part] = coarse_g(q, k).reshape(cchunk, B, full)

    def coarse_product(ext, r):
        base = p * n_c - RIM_C
        picked = [ext[place_of(jc[j, r] - base, all_c, ext.shape[0])] for j in range(NB)]
        return dot(vc[r], jnp.concatenate(picked, axis=0))

    def coarse_step(q, source, target, k):
        for i in range(cchunk):
            r = q * cchunk + i
            value = gc[k, r] + 2.0 * coarse_product(source, r)
            if k == 1:
                value = value - ce3[RIM_C + r].astype(F32)
            target[RIM_C + r] = value.astype(BF16)

    for i, (source, target, k) in enumerate(((ce3, ce2, 2), (ce2, ce1, 1))):
        turn_fine(2 * i, 2 * i + 2)
        with jax.named_scope(f"coarse halo {k}"):
            for copy in halos[-1]:
                copy.wait_recv()
        for q in (0, 1, n_c // cchunk - 2, n_c // cchunk - 1):
            coarse_step(q, source, target, k)
        halos.append(coarse_halo(i + 1, target))
        for copy in halos[-1]:
            copy.start()

        @pl.loop(2, n_c // cchunk - 2)
        def _(q, source=source, target=target, k=k):
            coarse_step(q, source, target, k)

    turn_fine(4, 6)
    with jax.named_scope("coarse halo 0"):
        for copy in halos[-1]:
            copy.wait_recv()
    with jax.named_scope("coarse last"):
        bias_c = jnp.concatenate([cb[0], cb[1]], axis=1)

        @pl.loop(0, n_c // cchunk)
        def _(q):
            for i in range(cchunk):
                r = q * cchunk + i
                value = gc[0, r] + coarse_product(ce1, r) - ce2[RIM_C + r].astype(F32)
                hidden[r] = jnp.maximum(value + bias_c, 0.0).astype(BF16)

    turn_fine(6, 8)

    for load in loads[4:]:
        load.wait()
    up_copy.wait_recv()
    sw_copy.wait_recv()

    def unpooled(q, k, slot):
        x = hidden[pl.ds(q * cchunk, cchunk)].reshape(crows, full)
        value = dot(x, up[k])
        for i in range(4):
            g[slot, pl.ds(4 * crows * q + i, crows, stride=4), :] = value

    with jax.named_scope("unpool"):
        @pl.loop(0, n_c // cchunk)
        def _(q):
            for k in range(1, TERMS):
                unpooled(q, k, k % 3)

    def fine_part(q):
        return pl.ds(pl.multiple_of(q * rows, rows), rows)

    def joined_g(q, k, slot):
        part = fine_part(q)
        x = jnp.concatenate([skip_own[part, :], skip_oth[part, :]], axis=1)
        return g[slot, part, :] + dot(x, sw[k])

    ends = 2 * RIM_F // chunk

    def put(q, values, own, lo, hi, place):
        blocks = pl.ds(q * chunk, chunk)
        own[blocks] = values
        if place == "lo":
            lo[pl.ds(RIM_F + q * chunk, chunk)] = values
        if place == "hi":
            hi[pl.ds((q - (steps - ends)) * chunk, chunk)] = values

    def fine_halo(i, lo, hi):
        sems = halo_f_sem.at[i]
        to_left = remote(
            lo.at[pl.ds(RIM_F, RIM_F)], hi.at[pl.ds(2 * RIM_F, RIM_F)], sems.at[0], left
        )
        to_right = remote(hi.at[pl.ds(RIM_F, RIM_F)], lo.at[pl.ds(0, RIM_F)], sems.at[1], right)
        return to_left, to_right

    def fine_first(q, place):
        skip_copy(q).wait_recv()
        values = joined_g(q, 3, 0).astype(BF16).reshape(chunk, B, half)
        put(q, values, b3, lo3, hi3, place)

    edge = RIM_F // chunk

    with jax.named_scope("fine first ends"):
        @pl.loop(0, edge)
        def _(q):
            fine_first(q, "lo")

        @pl.loop(steps - edge, steps)
        def _(q):
            fine_first(q, "hi")

    fine_halos = [fine_halo(0, lo3, hi3)]
    for copy in fine_halos[-1]:
        copy.start()

    with jax.named_scope("fine first"):
        @pl.loop(edge, ends)
        def _(q):
            fine_first(q, "lo")

        @pl.loop(steps - ends, steps - edge)
        def _(q):
            fine_first(q, "hi")

        @pl.loop(ends, steps - ends)
        def _(q):
            fine_first(q, None)

    with jax.named_scope("fine g"):
        @pl.loop(0, n_c // cchunk)
        def _(q):
            unpooled(q, 0, 0)

        @pl.loop(0, steps)
        def _(q):
            for k in range(TERMS - 1):
                value = joined_g(q, k, k)
                if k == 0:
                    value = value + fb[...]
                g[k, fine_part(q), :] = value

    def fine_product(source, first, r):
        base = p * n_f + first
        picked = [source[place_of(jf[j, r] - base, all_f, source.shape[0])] for j in range(NB)]
        return dot(vf[r], jnp.concatenate(picked, axis=0))

    def fine_step(q, k, source, first, place):
        for i in range(chunk):
            r = q * chunk + i
            part = pl.ds(pl.multiple_of(r * B, B), B)
            value = fine_product(source, first, r)
            if k == 0:
                value = g[0, part, :] + value - b2[r].astype(F32)
                out[part, :] = value.astype(BF16)
                continue
            value = g[k, part, :] + 2.0 * value
            if k == 1:
                value = value - b3[r].astype(F32)
            value = value.astype(BF16)
            own, lo, hi = ((b1, lo1, hi1), (b2, lo2, hi2))[k - 1]
            own[r] = value
            if place == "lo":
                lo[RIM_F + r] = value
            if place == "hi":
                hi[r - (n_f - 2 * RIM_F)] = value

    def out_copy(q):
        part = fine_part(q)
        return pltpu.make_async_copy(out.at[part], out_hbm.at[part], out_sem.at[q])

    sources = ((b3, lo3, hi3), (b2, lo2, hi2), (b1, lo1, hi1))
    for i, k in enumerate((2, 1, 0)):
        own, lo, hi = sources[i]

        def region(start, stop, source, first, place, k=k):
            @pl.loop(start, stop)
            def _(q):
                fine_step(q, k, source, first, place)
                if k == 0:
                    out_copy(q).start()

        with jax.named_scope(f"fine inner {k}"):
            region(edge, ends, own, 0, "lo")
            region(steps - ends, steps - edge, own, 0, "hi")
            region(ends, steps - ends, own, 0, None)
        with jax.named_scope(f"fine halo {k}"):
            for copy in fine_halos[-1]:
                copy.wait_recv()
        with jax.named_scope(f"fine border {k}"):
            region(0, edge, lo, -RIM_F, "lo")
            region(steps - edge, steps, hi, n_f - 2 * RIM_F, "hi")
        if k > 0:
            fine_halos.append(fine_halo(i + 1, *sources[i + 1][1:]))
            for copy in fine_halos[-1]:
                copy.start()

    with jax.named_scope("finish"):
        @pl.loop(0, steps)
        def _(q):
            skip_copy(q).wait_send()
            out_copy(q).wait()

        for pair in halos + fine_halos:
            for copy in pair:
                copy.wait_send()
        for copy in gathers[1:]:
            copy.wait_send()


def per_device(
    n_patch,
    coarse_map,
    skip_map,
    coarse_values,
    coarse_columns,
    fine_values,
    fine_columns,
    coarse_weight,
    coarse_bias,
    up_weight,
    skip_weight,
    fine_bias,
):
    pixels_c, half = coarse_map.shape
    pixels_f = skip_map.shape[0]
    width = coarse_values.shape[1]
    n_c, n_f = pixels_c // B, pixels_f // B
    full = 2 * half
    steps = n_f // 8
    anywhere = pl.BlockSpec(memory_space=pl.ANY)
    scalars = pl.BlockSpec(memory_space=pltpu.SMEM)
    vmem = pl.BlockSpec(memory_space=pltpu.VMEM)
    dma = pltpu.SemaphoreType.DMA
    border = pltpu.VMEM((3 * RIM_F, B, half), BF16)
    own = pltpu.VMEM((n_f, B, half), BF16)
    coarse_ext = pltpu.VMEM((n_c + 2 * RIM_C, B, full), BF16)
    return pl.pallas_call(
        functools.partial(kernel, n_patch),
        out_shape=jax.ShapeDtypeStruct((pixels_f, half), BF16),
        in_specs=[
            anywhere,
            anywhere,
            anywhere,
            scalars,
            anywhere,
            scalars,
            anywhere,
            anywhere,
            anywhere,
            anywhere,
            vmem,
        ],
        out_specs=anywhere,
        scratch_shapes=[
            pltpu.VMEM((pixels_c, half), BF16),
            pltpu.VMEM((pixels_c, half), BF16),
            pltpu.VMEM((n_c, B, width), BF16),
            pltpu.VMEM((TERMS, full, full), BF16),
            pltpu.VMEM((2, 1, half), F32),
            pltpu.VMEM((TERMS, full, half), BF16),
            pltpu.VMEM((TERMS, full, half), BF16),
            pltpu.VMEM((pixels_f, half), BF16),
            pltpu.VMEM((pixels_f, half), BF16),
            pltpu.VMEM((n_f, B, width), BF16),
            coarse_ext,
            coarse_ext,
            coarse_ext,
            pltpu.VMEM((TERMS - 1, n_c, B, full), F32),
            pltpu.VMEM((n_c, B, full), BF16),
            pltpu.VMEM((TERMS - 1, pixels_f, half), F32),
            own,
            own,
            own,
            border,
            border,
            border,
            border,
            border,
            border,
            pltpu.VMEM((pixels_f, half), BF16),
            pltpu.VMEM((width, pixels_c), BF16),
            pltpu.VMEM((2, width, 1024), BF16),
            dma((7,)),
            dma((2,)),
            dma((5, 2)),
            dma((steps, 2)),
            dma((3, 2, 2)),
            dma((3, 2, 2)),
            dma((steps,)),
        ],
        compiler_params=pltpu.CompilerParams(
            collective_id=0, has_side_effects=True, vmem_limit_bytes=63 * 1024 * 1024
        ),
    )(
        coarse_map,
        skip_map,
        coarse_values.T,
        coarse_columns.T,
        fine_values.T,
        fine_columns.T,
        coarse_weight,
        coarse_bias.reshape(1, half),
        up_weight,
        skip_weight,
        fine_bias.reshape(1, half),
    )


def solution(mesh):
    placed = (
        P("patch", "chan"),
        P("patch", "chan"),
        P("patch", None),
        P("patch", None),
        P("patch", None),
        P("patch", None),
        P(None, "chan", None),
        P("chan"),
        P(None, "chan", None),
        P(None, "chan", None),
        P("chan"),
    )
    return jax.shard_map(
        functools.partial(per_device, mesh.shape["patch"]),
        mesh=mesh,
        in_specs=placed,
        out_specs=P("patch", "chan"),
        check_vma=False,
    )
```

time: 518 us -> 111 us (0.21); the launches traced: 511 us -> 111 us
  local copies, waits for them, and re-layouts: 149 us -> 3.05 us
  waiting for transfers between devices: 129 us -> 0 us
  matrix products: 111 us -> 0 us
  Pallas kernels: 0 us -> 108 us
  other arithmetic: 60.1 us -> 0 us
  starting transfers between devices: 47.4 us -> 0 us
  between operations: 14 us -> 0.01 us
    gather x6 -> x0, local copies, waits for them, and re-layouts: 129 us -> none  [block_product(): picked = blocks[block_index].reshape(row_count, row_width, channels)]
    reduce_scatter x2 -> x0, waiting for transfers between devices: 125 us -> none  [the longest x1 103 us: per_device(): lax.psum_scatter(fine_terms, 'chan', scatter_dimension=1, tiled=True)]
    dot_general x14 -> x0, matrix products: 111 us -> none  [the longest x6 75.1 us: block_product(): jnp.einsum('rpq,rqc->rpc', entry_rows, picked, preferred_element_type=jnp...]
    pallas_call x0 -> x1, Pallas kernels: none -> 108 us  [per_device(): pl.pallas_call(functools.partial(kernel, n_patch), out_shape=jax.ShapeDty...]
    concatenate x7 -> x0, other arithmetic: 49.9 us -> none  [the longest x6 48.7 us: with_halo(): block = jnp.concatenate([low, block, high], axis=dim)]
    ppermute x12 -> x0, starting transfers between devices: 47.4 us -> none  [the longest x6 46.9 us: with_halo(): lax.ppermute(lax.slice_in_dim(block, 0, width, axis=dim), axis, backward)]
    unnamed x37 -> x1, local copies, waits for them, and re-layouts: 16.8 us -> 3.05 us
    convert_element_type x4 -> x0, other arithmetic: 9.48 us -> none  [the longest x2 4.28 us: chebyshev(): series.append(newer.astype(jnp.bfloat16))]
  transfers between devices with their start and end apart: 14 -> 0, of which waited for: 5 -> 0; matrix products, arithmetic and copies ran while one was open for 9% -> 0% of each run, Pallas kernels for 0% -> 0%
where the time goes in v1:
time: 111 us
  Pallas kernels  108 us (97%)
  local copies, waits for them, and re-layouts  3.05 us (3%)
    pallas_call x1, Pallas kernels, per_device(): pl.pallas_call(functools.partial(kernel, n_patch), out_shape=jax.ShapeDty...  108 us
    unnamed x1, local copies, waits for them, and re-layouts  3.05 us

profile of v1, /device:TPU:0, one launch (start us, length us, event | category | flops | bytes accessed | tf_op | source)
XLA Modules:
  0.0 111.1 jit_solution(8899099461042550665)
XLA Ops:
  0.0 108.0 %shard_map.109 = bf16[8192,128]{1,0:T(8,128)(2,1)} custom-call(bf16[2048,128]{1,0:T(8,128)(2,1)} %cm.1, bf16[8192,128]{1,0:T(8,128)(2,1)} %skip.1, bf16[576,2048]{1,0:T(8,128)(2,1)} %bitcast.7, s32[9,32]{1,0:T(8,128)} %bitcast.8, bf16[576,8192]{1,0:T(8,128)(2,1)} %bitcast.6, s32[9,128]{1,0:T(8,128)} %bitcast.9, bf16[4,128,256]{2,1,0:T(8,128)(2,1)} %wc_hbm.1, ...), custom_call_target="tpu_custom_call" | custom-call | tf_op jit(solution)/shard_map/pallas_call | solution.py:458
  108.0 3.0 %copy.13 = bf16[8192,128]{1,0:T(8,128)(2,1)} copy(bf16[8192,128]{1,0:T(8,128)(2,1)} %shard_map.109) | data formatting | bytes 4194304

commit v2 on v0

v2 whole, which is shorter than its diff:
```python
import functools

import jax
import jax.numpy as jnp
from jax import lax
from jax.experimental import pallas as pl
from jax.experimental.pallas import tpu as pltpu
from jax.sharding import PartitionSpec as P

B = 64
NB = 9
RIM_C = 8
RIM_F = 16
TERMS = 4
FLIP = 8
F32 = jnp.float32
BF16 = jnp.bfloat16
MESH = pl.DeviceIdType.MESH


def dot(a, b):
    return jnp.dot(a, b, preferred_element_type=F32)


def place_of(offset, blocks_all, held):
    return jnp.minimum(lax.bitwise_and(offset, blocks_all - 1), held - 1)


def kernel(
    n_patch,
    cm,
    skip,
    vc_hbm,
    jc,
    vf_hbm,
    jf,
    wc_hbm,
    cb_hbm,
    up_hbm,
    sw_hbm,
    fb,
    out,
    cm_own,
    cm_oth,
    vc,
    wc,
    cb,
    up,
    sw,
    skip_own,
    skip_oth,
    vf,
    turned,
    coarse_own,
    coarse_lo,
    coarse_hi,
    gc,
    hidden,
    g,
    fine_own,
    fine_lo,
    fine_hi,
    load_sem,
    turn_sem,
    gather_sem,
    skip_sem,
    halo_c_sem,
    halo_f_sem,
):
    p = lax.axis_index("patch")
    c = lax.axis_index("chan")
    left = (lax.rem(p + n_patch - 1, n_patch), c)
    right = (lax.rem(p + 1, n_patch), c)
    partner = (p, 1 - c)
    z_hi = lax.rem(p // FLIP, 2)
    far = (p + FLIP - 2 * FLIP * z_hi, 1 - c)

    n_c = vc.shape[0]
    n_f = vf.shape[0]
    all_c = n_c * n_patch
    all_f = n_f * n_patch
    half = cm.shape[1]
    full = 2 * half

    def remote(src, dst, sems, target):
        return pltpu.make_async_remote_copy(
            src_ref=src,
            dst_ref=dst,
            send_sem=sems.at[0],
            recv_sem=sems.at[1],
            device_id=target,
            device_id_type=MESH,
        )

    own_rows = pl.ds(pl.multiple_of(c * half, half), half)
    own_cols = own_rows
    far_cols = pl.ds(pl.multiple_of((1 - c) * half, half), half)

    lanes = 128
    cols = turned.shape[2]
    c_parts = n_c * B // cols
    f_parts = n_f * B // cols

    def entries(source, i, slot):
        part = pl.ds(pl.multiple_of(i * cols, cols), cols)
        return pltpu.make_async_copy(source.at[:, part], turned.at[slot], turn_sem.at[slot])

    def turn(target, i, slot):
        for t in range(cols // lanes):
            value = turned[slot, :, t * lanes : (t + 1) * lanes].T
            blocks = pl.ds(i * (cols // B) + t * (lanes // B), lanes // B)
            target[blocks] = value.reshape(lanes // B, B, value.shape[1])

    def turn_coarse():
        for i in range(c_parts):
            slot = i % 2
            entries(vc_hbm, i, slot).wait()
            turn(vc, i, slot)
            if i + 2 < c_parts:
                entries(vc_hbm, i + 2, slot).start()
            else:
                entries(vf_hbm, i + 2 - c_parts, slot).start()

    def turn_fine(start, stop):
        @pl.loop(start // 2, stop // 2)
        def _(pair):
            for slot in range(2):
                i = 2 * pair + slot
                entries(vf_hbm, i, slot).wait()
                turn(vf, i, slot)

                @pl.when(i + 2 < f_parts)
                def _():
                    entries(vf_hbm, i + 2, slot).start()

    pairs = [
        (cm, cm_own),
        (wc_hbm, wc.at[:, pl.ds(0, half), :]),
        (cb_hbm, cb.at[c]),
        (up_hbm.at[:, :, own_cols], up.at[:, own_rows, :]),
        (sw_hbm.at[:, :, own_cols], sw.at[:, pl.ds(0, half), :]),
        (skip, skip_own),
    ]
    loads = [pltpu.make_async_copy(a, b, load_sem.at[i]) for i, (a, b) in enumerate(pairs)]
    entries(vc_hbm, 0, 0).start()
    entries(vc_hbm, 1, 1).start()
    for load in loads:
        load.start()

    barrier = pltpu.get_barrier_semaphore()
    for target in (left, right, partner, far):
        pl.semaphore_signal(barrier, inc=1, device_id=target, device_id_type=MESH)
    pl.semaphore_wait(barrier, 4)

    cm_copy = remote(cm, cm_oth, gather_sem.at[0], partner)
    wc_copy = remote(wc_hbm, wc.at[:, pl.ds(half, half), :], gather_sem.at[1], far)
    cb_copy = remote(cb_hbm, cb.at[c], gather_sem.at[2], far)
    up_copy = remote(up_hbm.at[:, :, far_cols], up.at[:, own_rows, :], gather_sem.at[3], far)
    sw_copy = remote(
        sw_hbm.at[:, :, far_cols], sw.at[:, pl.ds(half, half), :], gather_sem.at[4], far
    )
    gathers = [cm_copy, wc_copy, cb_copy, up_copy, sw_copy]
    for copy in gathers:
        copy.start()

    chunk = 8
    steps = n_f // chunk
    rows = chunk * B

    def skip_copy(q):
        part = pl.ds(pl.multiple_of(q * rows, rows), rows)
        return remote(skip.at[part], skip_oth.at[part], skip_sem.at[q], partner)

    for load in loads[:3]:
        load.wait()
    turn_coarse()
    for copy in (wc_copy, cb_copy, cm_copy):
        copy.wait_recv()
    cm_copy.wait_send()

    def skip_send(*pair_numbers):
        for q in pair_numbers:
            skip_copy(q).start()
            skip_copy(steps - 1 - q).start()

    skip_send(0, 1)

    def coarse_keep(slot, r, values):
        coarse_own[slot][r] = values
        if r < n_c // 2:
            coarse_lo[slot][RIM_C + r] = values
        else:
            coarse_hi[slot][r - n_c // 2] = values

    def coarse_g(first, count, k):
        part = pl.ds(first * B, count * B)
        x = jnp.concatenate([cm_own[part, :], cm_oth[part, :]], axis=1)
        return dot(x, wc[k])

    def coarse_halo(slot):
        sems = halo_c_sem.at[slot]
        to_left = remote(
            coarse_lo[slot].at[pl.ds(RIM_C, RIM_C)],
            coarse_hi[slot].at[pl.ds(n_c // 2, RIM_C)],
            sems.at[0],
            left,
        )
        to_right = remote(
            coarse_hi[slot].at[pl.ds(n_c // 2 - RIM_C, RIM_C)],
            coarse_lo[slot].at[pl.ds(0, RIM_C)],
            sems.at[1],
            right,
        )
        return to_left, to_right

    def coarse_first(first):
        values = coarse_g(first, RIM_C, 3).astype(BF16).reshape(RIM_C, B, full)
        for i in range(RIM_C):
            coarse_keep(0, first + i, values[i])

    coarse_first(0)
    coarse_first(n_c - RIM_C)
    halos = [coarse_halo(0)]
    for copy in halos[-1]:
        copy.start()
    for first in range(RIM_C, n_c - RIM_C, RIM_C):
        coarse_first(first)

    @pl.loop(0, n_c // RIM_C)
    def _(q):
        part = pl.ds(pl.multiple_of(q * RIM_C * B, RIM_C * B), RIM_C * B)
        x = jnp.concatenate([cm_own[part, :], cm_oth[part, :]], axis=1)
        for k in range(TERMS - 1):
            value = dot(x, wc[k])
            gc[2 * k, part, :] = value[:, :half]
            gc[2 * k + 1, part, :] = value[:, half:]

    skip_send(2)
    bias_c = jnp.concatenate([cb[0], cb[1]], axis=1)

    def coarse_rows(slot, numbers):
        k = 2 - slot
        for r in numbers:
            if r < RIM_C:
                source, first = coarse_lo, -RIM_C
            elif r >= n_c - RIM_C:
                source, first = coarse_hi, n_c // 2
            else:
                source, first = coarse_own, 0
            base = p * n_c + first
            picked = [
                source[slot][place_of(jc[j, r] - base, all_c, source[slot].shape[0])] for j in range(NB)
            ]
            value = dot(vc[r], jnp.concatenate(picked, axis=0))
            part = pl.ds(r * B, B)
            term = jnp.concatenate([gc[2 * k, part, :], gc[2 * k + 1, part, :]], axis=1)
            if k > 0:
                value = 2.0 * value
            value = term + value
            if slot > 0:
                value = value - coarse_own[slot - 1][r].astype(F32)
            if k > 0:
                coarse_keep(slot + 1, r, value.astype(BF16))
            else:
                hidden[r] = jnp.maximum(value + bias_c, 0.0).astype(BF16)

    for slot in range(3):
        coarse_rows(slot, range(RIM_C, n_c - RIM_C))
        skip_send(3 + slot)
        turn_fine(slot * (f_parts // 4), (slot + 1) * (f_parts // 4))
        for copy in halos[-1]:
            copy.wait_recv()
        coarse_rows(slot, [*range(RIM_C), *range(n_c - RIM_C, n_c)])
        if slot < 2:
            halos.append(coarse_halo(slot + 1))
            for copy in halos[-1]:
                copy.start()

    for load in loads[3:]:
        load.wait()
    up_copy.wait_recv()
    sw_copy.wait_recv()
    quarter = gc.shape[1]

    @pl.loop(0, n_c // 4)
    def _(q):
        count = 4 * B
        x = hidden[pl.ds(q * 4, 4)].reshape(count, full)
        low = dot(x, jnp.concatenate([up[0], up[1]], axis=1))
        high = dot(x, jnp.concatenate([up[2], up[3]], axis=1))
        slot = 2 + (4 * count * q) // quarter
        start = (4 * count * q) % quarter
        for i in range(4):
            part = pl.ds(4 * count * q + i, count, stride=4)
            g[0, part, :] = low[:, :half] + fb[...]
            g[1, part, :] = low[:, half:]
            g[2, part, :] = high[:, :half]
            gc[slot, pl.ds(start + i, count, stride=4), :] = high[:, half:]

    skip_send(6)
    turn_fine(3 * (f_parts // 4), f_parts)
    skip_send(7)

    edge = RIM_F // chunk
    ends = 2 * edge

    def fine_keep(slot, near, i, r, values):
        fine_own[slot][r] = values
        if near == "lo":
            fine_lo[slot][RIM_F + r] = values
        if near == "hi":
            fine_hi[slot][r - (n_f - 2 * RIM_F)] = values

    def both(q, near):
        return ((q, "lo" if near else None), (steps - 1 - q, "hi" if near else None))

    def fine_first(q, near):
        for at, side in both(q, near):
            skip_copy(at).wait_recv()
        for at, side in both(q, near):
            part = pl.ds(pl.multiple_of(at * rows, rows), rows)
            x = jnp.concatenate([skip_own[part, :], skip_oth[part, :]], axis=1)
            low = dot(x, jnp.concatenate([sw[0], sw[1]], axis=1))
            high = dot(x, jnp.concatenate([sw[2], sw[3]], axis=1))
            g[0, part, :] += low[:, :half]
            g[1, part, :] += low[:, half:]
            g[2, part, :] += high[:, :half]
            slot = 2 + (at * rows) // quarter
            start = pl.multiple_of((at * rows) % quarter, rows)
            value = high[:, half:] + gc[slot, pl.ds(start, rows), :]
            value = value.astype(BF16).reshape(chunk, B, half)
            for i in range(chunk):
                fine_keep(0, side, i, at * chunk + i, value[i])

    def fine_halo(slot):
        sems = halo_f_sem.at[slot]
        to_left = remote(
            fine_lo[slot].at[pl.ds(RIM_F, RIM_F)],
            fine_hi[slot].at[pl.ds(2 * RIM_F, RIM_F)],
            sems.at[0],
            left,
        )
        to_right = remote(
            fine_hi[slot].at[pl.ds(RIM_F, RIM_F)],
            fine_lo[slot].at[pl.ds(0, RIM_F)],
            sems.at[1],
            right,
        )
        return to_left, to_right

    def fine_rows(slot, q, near, border=False):
        k = 2 - slot
        for at, side in both(q, near):
            if not border:
                source, first = fine_own, 0
            elif side == "lo":
                source, first = fine_lo, -RIM_F
            else:
                source, first = fine_hi, n_f - 2 * RIM_F
            base = p * n_f + first
            for i in range(chunk):
                r = at * chunk + i
                part = pl.ds(pl.multiple_of(r * B, B), B)
                picked = [
                    source[slot][place_of(jf[j, r] - base, all_f, source[slot].shape[0])]
                    for j in range(NB)
                ]
                value = dot(vf[r], jnp.concatenate(picked, axis=0))
                if k > 0:
                    value = 2.0 * value
                value = g[k, part, :] + value
                if slot > 0:
                    value = value - fine_own[slot - 1][r].astype(F32)
                value = value.astype(BF16)
                if k > 0:
                    fine_keep(slot + 1, side, i, r, value)
                else:
                    out[part, :] = value

    fine_halos = []

    def send(slot):
        fine_halos.append(fine_halo(slot))
        for copy in fine_halos[-1]:
            copy.start()

    def arrived(slot):
        for copy in fine_halos[slot]:
            copy.wait_recv()

    def run(start, stop, body):
        if stop - start == 1:
            body(start)
        else:
            pl.loop(start, stop)(body)

    def first_of(start, stop, near):
        run(start, stop, lambda q: fine_first(q, near))

    def rows_of(slot, start, stop, near, border=False):
        run(start, stop, lambda q: fine_rows(slot, q, near, border))

    middle = steps // 2
    first_of(0, edge, True)
    send(0)
    first_of(edge, ends, True)
    first_of(ends, ends + 2, False)
    rows_of(0, edge, ends, True)
    arrived(0)
    rows_of(0, 0, edge, True, True)
    send(1)
    first_of(ends + 2, ends + 3, False)
    rows_of(0, ends, ends + 1, False)
    first_of(ends + 3, middle, False)
    rows_of(0, ends + 1, middle, False)
    rows_of(1, ends, middle, False)
    arrived(1)
    rows_of(1, 0, edge, True, True)
    send(2)
    rows_of(1, edge, ends, True)
    rows_of(2, edge, middle, False)
    arrived(2)
    rows_of(2, 0, edge, True, True)

    @pl.loop(0, steps)
    def _(q):
        skip_copy(q).wait_send()

    for pair in halos + fine_halos:
        for copy in pair:
            copy.wait_send()
    for copy in gathers[1:]:
        copy.wait_send()


def per_device(
    n_patch,
    coarse_map,
    skip_map,
    coarse_values,
    coarse_columns,
    fine_values,
    fine_columns,
    coarse_weight,
    coarse_bias,
    up_weight,
    skip_weight,
    fine_bias,
):
    pixels_c, half = coarse_map.shape
    pixels_f = skip_map.shape[0]
    width = coarse_values.shape[1]
    n_c, n_f = pixels_c // B, pixels_f // B
    full = 2 * half
    steps = n_f // 8
    anywhere = pl.BlockSpec(memory_space=pl.ANY)
    scalars = pl.BlockSpec(memory_space=pltpu.SMEM)
    vmem = pl.BlockSpec(memory_space=pltpu.VMEM)
    dma = pltpu.SemaphoreType.DMA
    return pl.pallas_call(
        functools.partial(kernel, n_patch),
        out_shape=pltpu.VMEM((pixels_f, half), BF16),
        in_specs=[
            anywhere,
            anywhere,
            anywhere,
            scalars,
            anywhere,
            scalars,
            anywhere,
            anywhere,
            anywhere,
            anywhere,
            vmem,
        ],
        out_specs=vmem,
        scratch_shapes=[
            pltpu.VMEM((pixels_c, half), BF16),
            pltpu.VMEM((pixels_c, half), BF16),
            pltpu.VMEM((n_c, B, width), BF16),
            pltpu.VMEM((TERMS, full, full), BF16),
            pltpu.VMEM((2, 1, half), F32),
            pltpu.VMEM((TERMS, full, half), BF16),
            pltpu.VMEM((TERMS, full, half), BF16),
            pltpu.VMEM((pixels_f, half), BF16),
            pltpu.VMEM((pixels_f, half), BF16),
            pltpu.VMEM((n_f, B, width), BF16),
            pltpu.VMEM((2, width, 512), BF16),
            [pltpu.VMEM((n_c, B, full), BF16)] * 3,
            [pltpu.VMEM((n_c // 2 + RIM_C, B, full), BF16)] * 3,
            [pltpu.VMEM((n_c // 2 + RIM_C, B, full), BF16)] * 3,
            pltpu.VMEM((2 * (TERMS - 1), pixels_c, half), F32),
            pltpu.VMEM((n_c, B, full), BF16),
            pltpu.VMEM((TERMS - 1, pixels_f, half), F32),
            [pltpu.VMEM((n_f, B, half), BF16)] * 3,
            [pltpu.VMEM((3 * RIM_F, B, half), BF16)] * 3,
            [pltpu.VMEM((3 * RIM_F, B, half), BF16)] * 3,
            dma((6,)),
            dma((2,)),
            dma((5, 2)),
            dma((steps, 2)),
            dma((3, 2, 2)),
            dma((3, 2, 2)),
        ],
        compiler_params=pltpu.CompilerParams(
            collective_id=0, has_side_effects=True, vmem_limit_bytes=60 * 1024 * 1024
        ),
    )(
        coarse_map,
        skip_map,
        coarse_values.T,
        coarse_columns.T,
        fine_values.T,
        fine_columns.T,
        coarse_weight,
        coarse_bias.reshape(1, half),
        up_weight,
        skip_weight,
        fine_bias.reshape(1, half),
    )


def solution(mesh):
    placed = (
        P("patch", "chan"),
        P("patch", "chan"),
        P("patch", None),
        P("patch", None),
        P("patch", None),
        P("patch", None),
        P(None, "chan", None),
        P("chan"),
        P(None, "chan", None),
        P(None, "chan", None),
        P("chan"),
    )
    return jax.shard_map(
        functools.partial(per_device, mesh.shape["patch"]),
        mesh=mesh,
        in_specs=placed,
        out_specs=P("patch", "chan"),
        check_vma=False,
    )
```

time: 518 us -> 95.8 us (0.18); the launches traced: 511 us -> 95.5 us
  local copies, waits for them, and re-layouts: 149 us -> 1.32 us
  waiting for transfers between devices: 129 us -> 0 us
  matrix products: 111 us -> 0 us
  Pallas kernels: 0 us -> 94.2 us
  other arithmetic: 60.1 us -> 0 us
  starting transfers between devices: 47.4 us -> 0 us
  between operations: 14 us -> 0.01 us
    gather x6 -> x0, local copies, waits for them, and re-layouts: 129 us -> none  [block_product(): picked = blocks[block_index].reshape(row_count, row_width, channels)]
    reduce_scatter x2 -> x0, waiting for transfers between devices: 125 us -> none  [the longest x1 103 us: per_device(): lax.psum_scatter(fine_terms, 'chan', scatter_dimension=1, tiled=True)]
    dot_general x14 -> x0, matrix products: 111 us -> none  [the longest x6 75.1 us: block_product(): jnp.einsum('rpq,rqc->rpc', entry_rows, picked, preferred_element_type=jnp...]
    pallas_call x0 -> x1, Pallas kernels: none -> 94.2 us  [per_device(): pl.pallas_call(functools.partial(kernel, n_patch), out_shape=pltpu.VMEM((...]
    concatenate x7 -> x0, other arithmetic: 49.9 us -> none  [the longest x6 48.7 us: with_halo(): block = jnp.concatenate([low, block, high], axis=dim)]
    ppermute x12 -> x0, starting transfers between devices: 47.4 us -> none  [the longest x6 46.9 us: with_halo(): lax.ppermute(lax.slice_in_dim(block, 0, width, axis=dim), axis, backward)]
    unnamed x37 -> x1, local copies, waits for them, and re-layouts: 16.8 us -> 1.32 us
    convert_element_type x4 -> x0, other arithmetic: 9.48 us -> none  [the longest x2 4.28 us: chebyshev(): series.append(newer.astype(jnp.bfloat16))]
  transfers between devices with their start and end apart: 14 -> 0, of which waited for: 5 -> 0; matrix products, arithmetic and copies ran while one was open for 9% -> 0% of each run, Pallas kernels for 0% -> 0%
where the time goes in v2:
time: 95.8 us; the launch traced here: 95.5 us
  Pallas kernels  94.2 us (98%)
  local copies, waits for them, and re-layouts  1.32 us (1%)
    pallas_call x1, Pallas kernels, per_device(): pl.pallas_call(functools.partial(kernel, n_patch), out_shape=pltpu.VMEM((...  94.2 us

profile of v2, /device:TPU:0, one launch (start us, length us, event | category | flops | bytes accessed | tf_op | source)
XLA Modules:
  0.0 95.5 jit_solution(14487263399781715391)
XLA Ops:
  0.0 94.2 %shard_map.109 = bf16[8192,128]{1,0:T(8,128)(2,1)S(1)} custom-call(bf16[2048,128]{1,0:T(8,128)(2,1)} %cm.1, bf16[8192,128]{1,0:T(8,128)(2,1)} %skip.1, bf16[576,2048]{1,0:T(8,128)(2,1)} %bitcast.7, s32[9,32]{1,0:T(8,128)} %bitcast.8, bf16[576,8192]{1,0:T(8,128)(2,1)} %bitcast.6, s32[9,128]{1,0:T(8,128)} %bitcast.9, bf16[4,128,256]{2,1,0:T(8,128)(2,1)} %wc_hbm.1, ...), custom_call_target="tpu_custom_call" | custom-call | tf_op jit(solution)/shard_map/pallas_call | solution.py:460
  94.2 1.3 %copy.13 = bf16[8192,128]{1,0:T(8,128)(2,1)} copy(bf16[8192,128]{1,0:T(8,128)(2,1)S(1)} %shard_map.109) | data formatting | bytes 4194304

commit v3 on v2

--- a/solution.py
+++ b/solution.py
@@ -72,6 +72,9 @@
     left = (lax.rem(p + n_patch - 1, n_patch), c)
     right = (lax.rem(p + 1, n_patch), c)
     partner = (p, 1 - c)
+    row = lax.rem(p, FLIP)
+    coarse_left = (left[0], jnp.where(row == 0, 1 - c, c))
+    coarse_right = (right[0], jnp.where(row == FLIP - 1, 1 - c, c))
     z_hi = lax.rem(p // FLIP, 2)
     far = (p + FLIP - 2 * FLIP * z_hi, 1 - c)
 
@@ -148,9 +151,9 @@
         load.start()
 
     barrier = pltpu.get_barrier_semaphore()
-    for target in (left, right, partner, far):
+    for target in (left, right, coarse_left, coarse_right, partner, far):
         pl.semaphore_signal(barrier, inc=1, device_id=target, device_id_type=MESH)
-    pl.semaphore_wait(barrier, 4)
+    pl.semaphore_wait(barrier, 6)
 
     cm_copy = remote(cm, cm_oth, gather_sem.at[0], partner)
     wc_copy = remote(wc_hbm, wc.at[:, pl.ds(half, half), :], gather_sem.at[1], far)
@@ -203,13 +206,13 @@
             coarse_lo[slot].at[pl.ds(RIM_C, RIM_C)],
             coarse_hi[slot].at[pl.ds(n_c // 2, RIM_C)],
             sems.at[0],
-            left,
+            coarse_left,
         )
         to_right = remote(
             coarse_hi[slot].at[pl.ds(n_c // 2 - RIM_C, RIM_C)],
             coarse_lo[slot].at[pl.ds(0, RIM_C)],
             sems.at[1],
-            right,
+            coarse_right,
         )
         return to_left, to_right
 

time: 95.8 us -> 87.4 us (0.912)
  Pallas kernels: 94.2 us -> 85.8 us
    pallas_call x1, Pallas kernels: 94.2 us -> 85.8 us  [per_device(): pl.pallas_call(functools.partial(kernel, n_patch), out_shape=pltpu.VMEM((...]
where the time goes in v3:
time: 87.4 us; the launch traced here: 87.1 us
  Pallas kernels  85.8 us (98%)
  local copies, waits for them, and re-layouts  1.32 us (2%)
    pallas_call x1, Pallas kernels, per_device(): pl.pallas_call(functools.partial(kernel, n_patch), out_shape=pltpu.VMEM((...  85.8 us

profile of v3, /device:TPU:0, one launch (start us, length us, event | category | flops | bytes accessed | tf_op | source)
XLA Modules:
  0.0 87.1 jit_solution(3442267720768557298)
XLA Ops:
  0.0 85.8 %shard_map.109 = bf16[8192,128]{1,0:T(8,128)(2,1)S(1)} custom-call(bf16[2048,128]{1,0:T(8,128)(2,1)} %cm.1, bf16[8192,128]{1,0:T(8,128)(2,1)} %skip.1, bf16[576,2048]{1,0:T(8,128)(2,1)} %bitcast.7, s32[9,32]{1,0:T(8,128)} %bitcast.8, bf16[576,8192]{1,0:T(8,128)(2,1)} %bitcast.6, s32[9,128]{1,0:T(8,128)} %bitcast.9, bf16[4,128,256]{2,1,0:T(8,128)(2,1)} %wc_hbm.1, ...), custom_call_target="tpu_custom_call" | custom-call | tf_op jit(solution)/shard_map/pallas_call | solution.py:463
  85.8 1.3 %copy.13 = bf16[8192,128]{1,0:T(8,128)(2,1)} copy(bf16[8192,128]{1,0:T(8,128)(2,1)S(1)} %shard_map.109) | data formatting | bytes 4194304

commit v4 on v3

--- a/solution.py
+++ b/solution.py
@@ -174,6 +174,12 @@
         part = pl.ds(pl.multiple_of(q * rows, rows), rows)
         return remote(skip.at[part], skip_oth.at[part], skip_sem.at[q], partner)
 
+    def skip_send(*pair_numbers):
+        for q in pair_numbers:
+            skip_copy(q).start()
+            skip_copy(steps - 1 - q).start()
+
+    skip_send(0)
     for load in loads[:3]:
         load.wait()
     turn_coarse()
@@ -181,12 +187,7 @@
         copy.wait_recv()
     cm_copy.wait_send()
 
-    def skip_send(*pair_numbers):
-        for q in pair_numbers:
-            skip_copy(q).start()
-            skip_copy(steps - 1 - q).start()
-
-    skip_send(0, 1)
+    skip_send(1, 2)
 
     def coarse_keep(slot, r, values):
         coarse_own[slot][r] = values
@@ -238,7 +239,7 @@
             gc[2 * k, part, :] = value[:, :half]
             gc[2 * k + 1, part, :] = value[:, half:]
 
-    skip_send(2)
+    skip_send(3)
     bias_c = jnp.concatenate([cb[0], cb[1]], axis=1)
 
     def coarse_rows(slot, numbers):
@@ -269,7 +270,7 @@
 
     for slot in range(3):
         coarse_rows(slot, range(RIM_C, n_c - RIM_C))
-        skip_send(3 + slot)
+        skip_send(4 + slot)
         turn_fine(slot * (f_parts // 4), (slot + 1) * (f_parts // 4))
         for copy in halos[-1]:
             copy.wait_recv()
@@ -300,9 +301,8 @@
             g[2, part, :] = high[:, :half]
             gc[slot, pl.ds(start + i, count, stride=4), :] = high[:, half:]
 
-    skip_send(6)
+    skip_send(7)
     turn_fine(3 * (f_parts // 4), f_parts)
-    skip_send(7)
 
     edge = RIM_F // chunk
     ends = 2 * edge
@@ -414,13 +414,14 @@
     send(1)
     first_of(ends + 2, ends + 3, False)
     rows_of(0, ends, ends + 1, False)
-    first_of(ends + 3, middle, False)
-    rows_of(0, ends + 1, middle, False)
-    rows_of(1, ends, middle, False)
+    rows_of(1, edge, edge + 1, True)
     arrived(1)
     rows_of(1, 0, edge, True, True)
     send(2)
-    rows_of(1, edge, ends, True)
+    first_of(ends + 3, middle, False)
+    rows_of(0, ends + 1, middle, False)
+    rows_of(1, edge + 1, ends, True)
+    rows_of(1, ends, middle, False)
     rows_of(2, edge, middle, False)
     arrived(2)
     rows_of(2, 0, edge, True, True)

time: 87.4 us -> 83.6 us (0.957)
  Pallas kernels: 85.8 us -> 81.8 us
    pallas_call x1, Pallas kernels: 85.8 us -> 81.8 us  [per_device(): pl.pallas_call(functools.partial(kernel, n_patch), out_shape=pltpu.VMEM((...]
where the time goes in v4:
time: 83.6 us; the launch traced here: 83.2 us
  Pallas kernels  81.8 us (98%)
  local copies, waits for them, and re-layouts  1.32 us (2%)
    pallas_call x1, Pallas kernels, per_device(): pl.pallas_call(functools.partial(kernel, n_patch), out_shape=pltpu.VMEM((...  81.8 us

profile of v4, /device:TPU:0, one launch (start us, length us, event | category | flops | bytes accessed | tf_op | source)
XLA Modules:
  0.0 83.2 jit_solution(13494774941613859424)
XLA Ops:
  0.0 81.8 %shard_map.109 = bf16[8192,128]{1,0:T(8,128)(2,1)S(1)} custom-call(bf16[2048,128]{1,0:T(8,128)(2,1)} %cm.1, bf16[8192,128]{1,0:T(8,128)(2,1)} %skip.1, bf16[576,2048]{1,0:T(8,128)(2,1)} %bitcast.7, s32[9,32]{1,0:T(8,128)} %bitcast.8, bf16[576,8192]{1,0:T(8,128)(2,1)} %bitcast.6, s32[9,128]{1,0:T(8,128)} %bitcast.9, bf16[4,128,256]{2,1,0:T(8,128)(2,1)} %wc_hbm.1, ...), custom_call_target="tpu_custom_call" | custom-call | tf_op jit(solution)/shard_map/pallas_call | solution.py:464
  81.8 1.3 %copy.13 = bf16[8192,128]{1,0:T(8,128)(2,1)} copy(bf16[8192,128]{1,0:T(8,128)(2,1)S(1)} %shard_map.109) | data formatting | bytes 4194304
